TPU v7x, 512 devices: a whole 4x8x8 slice. The times are simulated.
512 devices in a mesh: region: 16 (over y, core), dev: 32 (over z, x).
Axes of the slice: x: 4, y: 8, z: 8, core: 2. Of those that a mesh axis runs over, the one named last changes fastest.
Arguments:
- data_panel: bfloat16 [64, 262144], P(None, ('region', 'dev'))
- reg_panel: bfloat16 [64, 524288], P(None, ('region', 'dev'))
- prev_panel: float32 [64, 524288], P(None, ('region', 'dev'))
- lower_block: float32 [64, 64], replicated
- sens_tiles: bfloat16 [4096, 8, 128, 128], P(('region', 'dev')), may hold values from -0.1875 to 0.1875
- sens_src: int32 [4096, 8], P(('region', 'dev')), may hold values from 0 to 31, as said below
- touched: int32 [16384], P(('region', 'dev')), may hold values from 0 to 3
- couple_tiles: bfloat16 [4096, 2, 128, 128], P(('region', 'dev')), may hold values from -0.375 to 0.375
- couple_map: int32 [4096, 2], P(('region', 'dev')), may hold values from 0 to 7
- grad_tiles: bfloat16 [4096, 3, 128, 128], P(('region', 'dev')), may hold values from -0.3125 to 0.3125
- grad_map: int32 [4096, 3], P(('region', 'dev')), may hold values from 0 to 9, as said below
Outputs:
- panel_q: float32 [64, 524288], P(None, ('region', 'dev'))
- factor: float32 [64, 64], replicated
Inputs may be any that keep to these rules, and one draw needn't show every extreme that they name: `sens_src`: on each device's 8 cell blocks every device index of the region appears at least once. `couple_map`: values below 4 name blocks of the region before, the others blocks of the region after. `grad_map`: the first column of local block i is i + 1 (the block itself), the others lie in i to i + 2; local block 0 reads value 0 and local block 7 reads value 8 + 1.
All inputs are finite; a program needn't handle non-finite values.
Results may differ from a plain program's by a relative error of at most 0.0029.
Values may be sent and summed in bfloat16 or wider, within the bound.
A program may use at most 64 MiB of HBM per device.

v0:
```python
import jax
import jax.numpy as jnp
from jax import lax
from jax.sharding import PartitionSpec as P

penalty_weight = 0.5


def extended_2(block, sides, width):
    for axis, dim in sides:
        count = lax.axis_size(axis)
        forward = [(i, i + 1) for i in range(count - 1)]
        backward = [(target, source) for source, target in forward]
        low = lax.ppermute(
            lax.slice_in_dim(block, block.shape[dim] - width, None, axis=dim), axis, forward
        )
        high = lax.ppermute(lax.slice_in_dim(block, 0, width, axis=dim), axis, backward)
        block = jnp.concatenate([low, block, high], axis=dim)
    return block


def tile_product(picked, tiles):
    return lax.dot_general(
        picked, tiles, (((2, 3), (1, 2)), ((1,), (0,))), preferred_element_type=jnp.float32
    )


def summed_gram(local_gram):
    return lax.psum(local_gram, ("region", "dev"))


def cholesky_pass(matrix, cell_total):
    gram_sum = summed_gram(jnp.dot(matrix, matrix.T, precision=lax.Precision.HIGHEST)) / cell_total
    lower_factor = jnp.linalg.cholesky(gram_sum)
    identity = jnp.eye(gram_sum.shape[0], dtype=jnp.float32)
    inverse = lax.linalg.triangular_solve(lower_factor, identity, left_side=True, lower=True)
    return (jnp.dot(inverse, matrix, precision=lax.Precision.HIGHEST), lower_factor)


def local(
    data_panel,
    reg_panel,
    prev_panel,
    lower_block,
    sens_tiles,
    sens_src,
    touched,
    couple_tiles,
    couple_map,
    grad_tiles,
    grad_map,
):
    panel_rows = data_panel.shape[0]
    block_len = sens_tiles.shape[-1]
    owned_cells = sens_tiles.shape[0]
    peer_count = lax.axis_size("dev")
    data_blocks = data_panel.shape[1] // block_len
    everyone = lax.all_gather(data_panel, "dev", axis=1, tiled=True).reshape(
        panel_rows, peer_count, data_blocks, block_len
    )
    compact = everyone[:, jnp.arange(peer_count), touched]
    direct = tile_product(compact[:, sens_src], sens_tiles)
    neighbours = extended_2(data_panel, (("region", 1),), data_blocks * block_len)
    neighbours = neighbours.reshape(panel_rows, 3 * data_blocks, block_len)
    remapped = jnp.where(couple_map < data_blocks, couple_map, couple_map + data_blocks)
    coupled = tile_product(neighbours[:, remapped], couple_tiles)
    extended = extended_2(reg_panel, ((("region", "dev"), 1),), block_len)
    extended = extended.reshape(panel_rows, owned_cells + 2, block_len)
    gradient = tile_product(extended[:, grad_map], grad_tiles)
    combined = direct + coupled + penalty_weight * gradient
    combined = jnp.transpose(combined, (1, 0, 2)).reshape(panel_rows, owned_cells * block_len)
    adjoint = combined - jnp.dot(lower_block, prev_panel, precision=lax.Precision.HIGHEST)
    cell_total = owned_cells * block_len * lax.axis_size("region") * peer_count
    first_q, first_lower = cholesky_pass(adjoint, cell_total)
    panel_q, second_lower = cholesky_pass(first_q, cell_total)
    factor = jnp.transpose(jnp.dot(first_lower, second_lower, precision=lax.Precision.HIGHEST))
    return (panel_q, factor)


def solution(mesh):
    return jax.shard_map(
        local,
        mesh=mesh,
        in_specs=(
            P(None, ("region", "dev")),
            P(None, ("region", "dev")),
            P(None, ("region", "dev")),
            P(),
            P(("region", "dev"), None, None, None),
            P(("region", "dev"), None),
            P(("region", "dev")),
            P(("region", "dev"), None, None, None),
            P(("region", "dev"), None),
            P(("region", "dev"), None, None, None),
            P(("region", "dev"), None),
        ),
        out_specs=(P(None, ("region", "dev")), P()),
        check_vma=False,
    )
```

profile of v0, /device:TPU:1, one launch (start us, length us, event | category | flops | bytes accessed | tf_op | source)
XLA Modules:
  0.0 342.4 jit_solution(11440855158909949903)
XLA Ops:
  7.9 4.6 %collective-permute-start = (bf16[64,512]{1,0:T(8,128)(2,1)}, bf16[64,512]{1,0:T(8,128)(2,1)S(1)}, u32[]{:S(2)}, u32[]{:S(2)}) collective-permute-start(bf16[64,512]{1,0:T(8,128)(2,1)} %param.14), channel_id=1, source_target_pairs={{0,32},{32,64},{64,96},{96,128},{128,160},{160,192},{192,224},{224... | collective-permute-start | bytes 196616 | tf_op jit(solution)/shard_map/ppermute | solution.py:14
  12.5 5.5 %collective-permute-start.1 = (bf16[64,512]{1,0:T(8,128)(2,1)}, bf16[64,512]{1,0:T(8,128)(2,1)S(1)}, u32[]{:S(2)}, u32[]{:S(2)}) collective-permute-start(bf16[64,512]{1,0:T(8,128)(2,1)} %param.14), channel_id=1, source_target_pairs={{32,0},{64,32},{96,64},{128,96},{160,128},{192,160},{224,192},{256... | collective-permute-start | bytes 196616 | tf_op jit(solution)/shard_map/ppermute | solution.py:17
  18.0 0.7 fusion.32
  18.8 1.9 collective-permute-start.2
  20.7 7.2 %collective-permute-start.3 = (bf16[64,128]{1,0:T(8,128)(2,1)S(1)}, bf16[64,128]{1,0:T(8,128)(2,1)S(1)}, u32[]{:S(2)}, u32[]{:S(2)}) collective-permute-start(bf16[64,128]{1,0:T(8,128)(2,1)S(1)} %get-tuple-element.5), channel_id=1, source_target_pairs={{1,0},{2,1},{3,2},{4,3},{5,4},{6,5},{7,6},{8,7},{9,8},{10,9},{11,1... | collective-permute-start | bytes 49160 | tf_op jit(solution)/shard_map/ppermute | solution.py:17
  29.6 0.7 compare_select_fusion
  31.1 0.9 copy_bitcast_fusion.1
  32.7 0.9 copy_bitcast_fusion
  34.2 60.2 %all-gather.2.cloned.1.call-done = bf16[64,16384]{1,0:T(8,128)(2,1)} async-done(((bf16[64,512]{1,0:T(8,128)(2,1)}), bf16[64,16384]{1,0:T(8,128)(2,1)}) %all-gather.2.cloned.1.call-update) | async-done | bytes 2097168 | tf_op jit(solution)/shard_map/all_gather | solution.py:58
  94.4 4.4 %reshape.27 = bf16[64,32,4,128]{3,2,1,0:T(4,128)(2,1)} reshape(bf16[64,16384]{1,0:T(8,128)(2,1)} %all-gather.2.cloned.1.call-done) | data formatting | bytes 4194304 | tf_op jit(solution)/shard_map/reshape | solution.py:58
  98.8 5.3 %copy.31 = bf16[64,32,4,128]{3,0,2,1:T(8,128)(2,1)} copy(bf16[64,32,4,128]{3,2,1,0:T(4,128)(2,1)} %reshape.27) | data formatting | bytes 4194304 | tf_op jit(solution)/shard_map/reshape | solution.py:58
  104.2 2.3 gather_fusion
  106.4 1.7 gather_fusion.1
  108.1 1.9 convolution_bitcast_fusion.2
  111.7 100.3 %psum.14 = f32[64,64]{0,1:T(8,128)S(1)} all-reduce(f32[64,64]{0,1:T(8,128)S(1)} %fusion.33), channel_id=1, replica_groups=mesh['region'=16,'dev'=32] {'region','dev'}, use_global_device_ids=true, to_apply=%region_0.1 | all-reduce | flops 4096 | bytes 32768 | tf_op jit(solution)/shard_map/psum | solution.py:29
  212.0 5.8 %cholesky.44 = f32[64,64]{1,0:T(8,128)S(1)} custom-call(f32[64,64]{1,0:T(8,128)S(1)} %fusion.11), custom_call_target="Cholesky" | custom-call | tf_op jit(solution)/shard_map/jit(cholesky)/cholesky | solution.py:34
  219.2 4.9 %custom-call.8 = f32[1,64,64]{1,2,0:T(8,128)S(1)} custom-call(f32[1,64,64]{2,1,0:T(8,128)S(1)} %fusion.15), custom_call_target="InvertDiagBlocksLowerTriangular" | custom-call | tf_op jit(solution)/shard_map/triangular_solve/custom-call.0 | solution.py:36
  225.1 94.7 %psum.15 = f32[64,64]{0,1:T(8,128)S(1)} all-reduce(f32[64,64]{0,1:T(8,128)S(1)} %fusion.35), channel_id=1, replica_groups=mesh['region'=16,'dev'=32] {'region','dev'}, use_global_device_ids=true, to_apply=%region_3.6 | all-reduce | flops 4096 | bytes 32768 | tf_op jit(solution)/shard_map/psum | solution.py:29
  319.9 5.8 %cholesky.55 = f32[64,64]{1,0:T(8,128)S(1)} custom-call(f32[64,64]{1,0:T(8,128)S(1)} %fusion.9), custom_call_target="Cholesky" | custom-call | tf_op jit(solution)/shard_map/jit(cholesky)/cholesky | solution.py:34
  325.8 0.7 compare_reduce_fusion
  326.5 2.2 fusion.18
  328.7 0.7 select_bitcast_fusion
  329.4 4.9 %custom-call.9 = f32[1,64,64]{1,2,0:T(8,128)S(1)} custom-call(f32[1,64,64]{2,1,0:T(8,128)S(1)} %select_bitcast_fusion), custom_call_target="InvertDiagBlocksLowerTriangular" | custom-call | tf_op jit(solution)/shard_map/triangular_solve/custom-call.0 | solution.py:36
  334.5 1.1 fusion.36
  (47 shorter events, 8.8 us)
Async XLA Ops:
  7.2 100.9 %copy-start = (bf16[8,8,128,128]{3,2,1,0:T(8,128)(2,1)S(1)}, bf16[8,8,128,128]{3,2,1,0:T(8,128)(2,1)}, u32[]{:S(2)}) copy-start(bf16[8,8,128,128]{3,2,1,0:T(8,128)(2,1)} %param.18) | copy-start | bytes 6291460
  7.2 87.2 %all-gather.2.cloned.1.call-start = ((), (), s32[]{:S(2)}) async-start(), calls=%async_computation | async-start | bytes 2162688 | tf_op jit(solution)/shard_map/all_gather | solution.py:58
  7.9 24.7 %collective-permute-start = (bf16[64,512]{1,0:T(8,128)(2,1)}, bf16[64,512]{1,0:T(8,128)(2,1)S(1)}, u32[]{:S(2)}, u32[]{:S(2)}) collective-permute-start(bf16[64,512]{1,0:T(8,128)(2,1)} %param.14), channel_id=1, source_target_pairs={{0,32},{32,64},{64,96},{96,128},{128,160},{160,192},{192,224},{224... | collective-permute-start | bytes 196616 | tf_op jit(solution)/shard_map/ppermute | solution.py:14
  12.5 20.1 %collective-permute-start.1 = (bf16[64,512]{1,0:T(8,128)(2,1)}, bf16[64,512]{1,0:T(8,128)(2,1)S(1)}, u32[]{:S(2)}, u32[]{:S(2)}) collective-permute-start(bf16[64,512]{1,0:T(8,128)(2,1)} %param.14), channel_id=1, source_target_pairs={{32,0},{64,32},{96,64},{128,96},{160,128},{192,160},{224,192},{256... | collective-permute-start | bytes 196616 | tf_op jit(solution)/shard_map/ppermute | solution.py:17
  18.8 12.3 %collective-permute-start.2 = (bf16[64,128]{1,0:T(8,128)(2,1)S(1)}, bf16[64,128]{1,0:T(8,128)(2,1)S(1)}, u32[]{:S(2)}, u32[]{:S(2)}) collective-permute-start(bf16[64,128]{1,0:T(8,128)(2,1)S(1)} %get-tuple-element.4), channel_id=1, source_target_pairs={{0,1},{1,2},{2,3},{3,4},{4,5},{5,6},{6,7},{7,8},{8,9},{9,10},{10,1... | collective-permute-start | bytes 49160 | tf_op jit(solution)/shard_map/ppermute | solution.py:14
  20.7 10.4 %collective-permute-start.3 = (bf16[64,128]{1,0:T(8,128)(2,1)S(1)}, bf16[64,128]{1,0:T(8,128)(2,1)S(1)}, u32[]{:S(2)}, u32[]{:S(2)}) collective-permute-start(bf16[64,128]{1,0:T(8,128)(2,1)S(1)} %get-tuple-element.5), channel_id=1, source_target_pairs={{1,0},{2,1},{3,2},{4,3},{5,4},{6,5},{7,6},{8,7},{9,8},{10,9},{11,1... | collective-permute-start | bytes 49160 | tf_op jit(solution)/shard_map/ppermute | solution.py:17
  108.1 1.9 copy-start.2
  108.1 2.1 copy-start.1
  110.0 1.0 copy-start.3
  110.0 0.9 copy-start.4
Sparse Core Ops, SparseCore 0:
  11.1 83.2 all-gather.1
where the time goes:
time: 343 us; the launch traced here: 342 us
  blocking collectives  195 us (57%)
  waiting for transfers between devices  60.9 us (18%)
  other arithmetic  28.9 us (8%)
  starting transfers between devices  19.2 us (6%)
  local copies, waits for them, and re-layouts  16.6 us (5%)
  between operations  14.3 us (4%)
  matrix products  7.56 us (2%)
    psum x2, blocking collectives, summed_gram(): return lax.psum(local_gram, ('region', 'dev'))  195 us
    all_gather x1, waiting for transfers between devices, local(): lax.all_gather(data_panel, 'dev', axis=1, tiled=True)  60.2 us
    another operation x6, other arithmetic, cholesky_pass(): lower_factor = jnp.linalg.cholesky(gram_sum)  13.1 us
    ppermute x2, starting transfers between devices, extended_2(): lax.ppermute(lax.slice_in_dim(block, 0, width, axis=dim), axis, backward)  12.7 us
    another operation x4, other arithmetic, cholesky_pass(): lax.linalg.triangular_solve(lower_factor, identity, left_side=True, lower...  11.1 us
    reshape x2, local copies, waits for them, and re-layouts, local(): lax.all_gather(data_panel, 'dev', axis=1, tiled=True)  9.76 us
  transfers between devices with their start and end apart: 5, of which 1 were waited for; matrix products, arithmetic and copies ran while one was open for 2% of the time, Pallas kernels for 0%

commit v1 on v0

v1 whole, which is shorter than its diff:
```python
import functools

import jax
import jax.numpy as jnp
from jax import lax
from jax.experimental import pallas as pl
from jax.experimental.pallas import tpu as pltpu
from jax.sharding import PartitionSpec as P

F32 = jnp.float32
BF16 = jnp.bfloat16
SLICES = 4
BLK = 128
X_CHIPS = 4


def two_sum(a, b):
    s = a + b
    t = s - a
    return s, (a - (s - t)) + (b - t)


def cut(value, sigma):
    top = (value + sigma) - sigma
    return top, value - top


def eliminate(aug, rows):
    blocks = [aug[8 * b : 8 * b + 8, :] for b in range(rows // 8)]
    sub = lax.broadcasted_iota(jnp.int32, (8, 128), 0)
    out = []
    for b in range(rows // 8):
        live = len(blocks)
        cols = [
            [jnp.broadcast_to(blk[:, 8 * b + k : 8 * b + k + 1], (8, 128)) for blk in blocks]
            for k in range(8)
        ]
        head = blocks[0]
        pivots = jnp.ones((8, 128), F32)
        for k in range(8):
            pivot = jnp.broadcast_to(cols[k][0][k : k + 1, :], (8, 128))
            inv = 1.0 / pivot
            pivots = jnp.where(sub == k, pivot, pivots)
            factor = [c * inv for c in cols[k]]
            factor[0] = jnp.where(sub > k, factor[0], 0.0)
            for m in range(k + 1, 8):
                across = jnp.broadcast_to(cols[m][0][k : k + 1, :], (8, 128))
                cols[m] = [c - f * across for c, f in zip(cols[m], factor)]
            row = jnp.broadcast_to(head[k : k + 1, :], (8, 128))
            head = head - factor[0] * row
            blocks = [head] + [blk - f * row for blk, f in zip(blocks[1:], factor[1:])]
        root = lax.rsqrt(pivots)
        root = root * (1.5 - (0.5 * pivots) * (root * root))
        out.append(head * root)
        blocks = blocks[1:]
    return jnp.concatenate(out, axis=0)


def split3(v):
    hi = v.astype(BF16)
    r = v - hi.astype(F32)
    mid = r.astype(BF16)
    return hi, mid, (r - mid.astype(F32)).astype(BF16)


def finish_kernel(g_ref, s_ref, q_ref, f_ref):
    n = 64
    g = g_ref[...]
    lane = lax.broadcasted_iota(jnp.int32, (n, 128), 1)
    subl = lax.broadcasted_iota(jnp.int32, (n, 128), 0)
    left = lane < n
    eye_right = (lane == subl + n).astype(F32)
    eye = (lane == subl).astype(F32)
    low_part = jnp.where(left, pltpu.roll(g, n, 1), 0.0)
    hi_part = jnp.where(left, g, 0.0)
    first = eliminate(hi_part + eye_right, n)

    w = jnp.where(left, pltpu.roll(first, n, 1), 0.0)
    wsig = jnp.max(jnp.abs(w), axis=1, keepdims=True) * 131072.0
    gsig = jnp.max(jnp.abs(hi_part), axis=0, keepdims=True) * 131072.0
    ws = []
    r = w
    for i in range(4):
        top, r = cut(r, wsig * (2.0 ** (-7 * i)))
        ws.append(top.astype(BF16)[:, :n])
    gs = []
    r = hi_part
    for i in range(3):
        top, r = cut(r, gsig * (2.0 ** (-7 * i)))
        gs.append(top.astype(BF16))
    r = r + low_part
    for i in range(3, 6):
        top, r = cut(r, gsig * (2.0 ** (-7 * i)))
        gs.append(top.astype(BF16))
    hi = lo = None
    for level in range(6):
        pairs = [(i, level - i) for i in range(4) if 0 <= level - i < 6]
        lhs = jnp.concatenate([ws[i] for i, _ in pairs], axis=1)
        rhs = jnp.concatenate([gs[j] for _, j in pairs], axis=0)
        term = jnp.dot(lhs, rhs, preferred_element_type=F32)
        if hi is None:
            hi, lo = term, jnp.zeros_like(term)
        else:
            hi, e = two_sum(hi, term)
            lo = lo + e
    t = hi + lo
    g2 = lax.dot_general(
        t, w, (((1,), (1,)), ((), ())), precision=lax.Precision.HIGHEST, preferred_element_type=F32
    )
    zero = jnp.zeros((n, n), F32)
    second = eliminate(jnp.concatenate([g2, zero], axis=1) + eye_right, n)
    w2 = jnp.where(left, pltpu.roll(second, n, 1), 0.0)
    both = jnp.dot(second[:, :n], first[:, :n], precision=lax.Precision.HIGHEST, preferred_element_type=F32)
    f_ref[...] = both
    m = jnp.dot(w2[:, :n], w[:, :n], precision=lax.Precision.HIGHEST, preferred_element_type=F32)
    parts = jnp.concatenate([jnp.concatenate([p] * SLICES, axis=1) for p in split3(m)], axis=0)
    for c in range(4):
        res = jnp.dot(parts, s_ref[:, 256 * c : 256 * c + 256], preferred_element_type=F32)
        q_ref[:, 256 * c : 256 * c + 256] = res[:n] + (res[n : 2 * n] + res[2 * n :])


def finish(g, s):
    vm = pl.BlockSpec(memory_space=pltpu.VMEM)
    return pl.pallas_call(
        finish_kernel,
        out_shape=(jax.ShapeDtypeStruct((64, 1024), F32), jax.ShapeDtypeStruct((64, 64), F32)),
        in_specs=[vm, vm],
        out_specs=(vm, vm),
        compiler_params=pltpu.CompilerParams(vmem_limit_bytes=32 * 2**20),
        name="finish",
    )(g, s)


def gram_local(a):
    n = 64
    sig = jnp.max(jnp.abs(a), axis=1, keepdims=True) * 131072.0
    parts = []
    r = a
    for i in range(SLICES):
        top, r = cut(r, sig * (2.0 ** (-7 * i)))
        parts.append(top.astype(BF16))
    s = jnp.concatenate(parts, axis=0)
    p = lax.dot_general(s, s, (((1,), (1,)), ((), ())), preferred_element_type=F32)
    order = [(0, 0), (1, 0), (0, 1), (2, 0), (1, 1), (3, 0), (2, 1), (3, 1)]
    hi = lo = None
    for i, h in order:
        term = p[n * i : n * i + n, 128 * h : 128 * h + 128]
        if hi is None:
            hi, lo = term, jnp.zeros_like(term)
        else:
            hi, e = two_sum(hi, term)
            lo = lo + e
    hi, e = two_sum(hi, pltpu.roll(hi, n, 1))
    lo = (lo + pltpu.roll(lo, n, 1)) + e
    hi, lo = hi + lo, lo - ((hi + lo) - hi)
    lane = lax.broadcasted_iota(jnp.int32, (n, 128), 1)
    return s, jnp.where(lane < n, hi, pltpu.roll(lo, n, 1))


MESH = pl.DeviceIdType.MESH


def gather_kernel(
    sizes,
    data, reg, prev, low, touched_any, touched, sens, src, couple, cmap, grad, gmap,
    s_out, g_out,
    zbs, compact, xs, nb, ext, prev_v, sens_v, couple_v, grad_v, asked, adj, s_v, gpart, rs, zs, ys, ag,
    l_sem, z_send, z_recv, x_send, x_recv, n_send, n_recv, t_send, t_recv, a_send, a_recv,
):
    xn, zn, rn, nbl, dbl, kk, kc, kg = sizes
    n = 64
    yn, gn = rn // 2, 2 * xn
    dn = xn * zn
    rows = n // gn
    half = zn // 2
    r = lax.axis_index("region")
    d = lax.axis_index("dev")
    y, core = r // 2, r % 2
    z, x = d // xn, d % xn
    piece = x * 2 + core

    mine = zbs[0]
    below = [mine] + list(zbs[1:half])
    above = [mine] + list(zbs[half : 2 * half - 1])
    across = zbs[2 * half - 1]

    local = []

    def fetch(source, target):
        c = pltpu.make_async_copy(source, target, l_sem.at[len(local)])
        c.start()
        local.append(c)
        return c

    own = [fetch(data.at[:, pl.ds(BLK * b, BLK)], mine.at[b]) for b in range(dbl)]
    rim = [fetch(reg.at[:, pl.ds(BLK * b, BLK)], ext.at[b + 1]) for b in range(nbl)]
    prev_c = fetch(prev, prev_v)
    grad_c = fetch(grad, grad_v)
    couple_c = fetch(couple, couple_v)
    sens_c = fetch(sens, sens_v)

    def group(o):
        q = (piece + o) % gn
        return (y * 2 + q % 2, z * xn + q // 2)

    def along_z(o):
        return (r, ((z + o) % zn) * xn + x)

    def along_y(o):
        return (((y + o) % yn) * 2 + core, d)

    def along_x(o):
        return (r, z * xn + (x + o) % xn)

    up, down = ((r + 1) % rn, d), ((r + rn - 1) % rn, d)
    g = r * dn + d
    g_up, g_down = (g + 1) % (rn * dn), (g + rn * dn - 1) % (rn * dn)
    after, before = (g_up // dn, g_up % dn), (g_down // dn, g_down % dn)
    reached = [group(o) for o in range(1, gn)] + [along_z(o) for o in range(1, zn)]
    reached += [along_y(o) for o in range(1, yn)] + [up, down, after, before]
    barrier = pltpu.get_barrier_semaphore()
    for who in reached:
        pl.semaphore_signal(barrier, inc=1, device_id=who, device_id_type=MESH)
    pl.semaphore_wait(barrier, len(reached))

    def remote(source, target, send, recv, who):
        c = pltpu.make_async_remote_copy(
            src_ref=source, dst_ref=target, send_sem=send, recv_sem=recv,
            device_id=who, device_id_type=MESH,
        )
        c.start()
        return c

    sent = []
    asks = []
    for o in range(1, xn):
        asks.append(remote(touched_any, asked.at[xn - o - 1], t_send.at[o - 1], t_recv.at[o - 1], along_x(o)))
    sent += asks
    for c in own:
        c.wait()

    def ring(step):
        mid = dbl // 2
        if step < half - 1:
            pairs = [(below[step], below[step + 1]), (above[step], above[step + 1])]
        else:
            low_half, high_half = pl.ds(0, mid), pl.ds(mid, dbl - mid)
            pairs = [(below[step].at[low_half], across.at[low_half]), (above[step].at[high_half], across.at[high_half])]
        return [
            remote(source, target, z_send.at[way, step], z_recv.at[way, step], along_z(1 if way == 0 else zn - 1))
            for way, (source, target) in enumerate(pairs)
        ]

    x_copies = []

    def hand_on(slot, zz, held):
        for o in range(1, xn):
            xs[o - 1, slot] = held[asked[o - 1, 0, zz * xn + x]]
            x_copies.append(
                remote(xs.at[o - 1, slot], compact.at[zz * xn + x],
                       x_send.at[o - 1, slot], x_recv.at[o - 1, slot], along_x(o))
            )
        compact[zz * xn + x] = held[touched[zz * xn + x]]

    moves = ring(0)
    sent += moves
    for c in rim:
        c.wait()
    near = [
        remote(mine, nb.at[pl.ds(0, dbl)], n_send.at[0], n_recv.at[0], up),
        remote(mine, nb.at[pl.ds(dbl, dbl)], n_send.at[1], n_recv.at[1], down),
        remote(ext.at[nbl], ext.at[0], n_send.at[2], n_recv.at[2], after),
        remote(ext.at[1], ext.at[nbl + 1], n_send.at[3], n_recv.at[3], before),
    ]
    sent += near
    for c in asks:
        c.wait_recv()
    hand_on(0, z, mine)

    prev_c.wait()
    adj[...] = -jnp.dot(low[...], prev_v[...], precision=lax.Precision.HIGHEST, preferred_element_type=F32)

    def gradient(first, last):
        for b in range(first, last):
            lhs = jnp.concatenate([ext[gmap[b, j]] for j in range(kg)], axis=1)
            part = jnp.dot(lhs, grad_v[b].reshape(kg * BLK, BLK), preferred_element_type=F32)
            adj[:, BLK * b : BLK * b + BLK] += 0.5 * part

    def coupling(first, last):
        for b in range(first, last):
            lhs = jnp.concatenate([nb[cmap[b, j]] for j in range(kc)], axis=1)
            part = jnp.dot(lhs, couple_v[b].reshape(kc * BLK, BLK), preferred_element_type=F32)
            adj[:, BLK * b : BLK * b + BLK] += part

    for step in range(half):
        for c in moves:
            c.wait_recv()
        if step < half - 1:
            moves = ring(step + 1)
            sent += moves
            hand_on(2 * step + 1, (z + zn - step - 1) % zn, below[step + 1])
            hand_on(2 * step + 2, (z + step + 1) % zn, above[step + 1])
        else:
            hand_on(zn - 1, (z + half) % zn, across)
        if step == 0:
            grad_c.wait()
            couple_c.wait()
            for c in near:
                c.wait_recv()

            @pl.when(g == 0)
            def _():
                ext[0] = jnp.zeros((n, BLK), BF16)

            @pl.when(g == rn * dn - 1)
            def _():
                ext[nbl + 1] = jnp.zeros((n, BLK), BF16)

            @pl.when(r == 0)
            def _():
                nb[pl.ds(0, dbl)] = jnp.zeros((dbl, n, BLK), BF16)

            @pl.when(r == rn - 1)
            def _():
                nb[pl.ds(dbl, dbl)] = jnp.zeros((dbl, n, BLK), BF16)

            gradient(0, nbl)
            coupling(0, nbl)
    sens_c.wait()
    for c in x_copies:
        c.wait_recv()
    for b in range(nbl):
        lhs = jnp.concatenate([compact[src[b, k]] for k in range(kk)], axis=1)
        part = jnp.dot(lhs, sens_v[b].reshape(kk * BLK, BLK), preferred_element_type=F32)
        adj[:, BLK * b : BLK * b + BLK] += part

    s, gram = gram_local(adj[...])
    s_v[...] = s
    s_copy = fetch(s_v, s_out)
    gram = gram * (1.0 / (rn * dn * nbl * BLK))
    for q in range(gn):
        gpart[q] = gram[rows * q : rows * q + rows, :]

    lane = lax.broadcasted_iota(jnp.int32, (rows, BLK), 1)

    def total(ref, count):
        hi = ref[0]
        lo = jnp.zeros_like(hi)
        for q in range(1, count):
            hi, e = two_sum(hi, ref[q])
            lo = lo + e
        lo = jnp.where(lane < n, lo, hi)
        hi_part = hi
        low_sum = pltpu.roll(lo, n, 1)
        tail = jnp.where(lane < n, low_sum, 0.0) + jnp.where(lane < n, lo, 0.0)
        top = jnp.where(lane < n, hi_part, 0.0)
        big = top + tail
        rest = tail - (big - top)
        return jnp.where(lane < n, big, pltpu.roll(rest, n, 1))

    def exchange(stage, count, mine, box, who, source):
        copies = []
        for o in range(1, count):
            copies.append(
                remote(source(o), box.at[mine], a_send.at[stage, o - 1], a_recv.at[stage, o - 1], who(o))
            )
        return copies

    copies = exchange(0, gn, piece, rs, group, lambda o: gpart.at[(piece + o) % gn])
    rs[piece] = gpart[piece]
    for c in copies:
        c.wait_recv()
    sent += copies
    zs[z] = total(rs, gn)
    copies = exchange(1, zn, z, zs, along_z, lambda o: zs.at[z])
    for c in copies:
        c.wait_recv()
    sent += copies
    ys[y] = total(zs, zn)
    copies = exchange(2, yn, y, ys, along_y, lambda o: ys.at[y])
    for c in copies:
        c.wait_recv()
    sent += copies
    ag[piece] = total(ys, yn)
    copies = exchange(3, gn, piece, ag, group, lambda o: ag.at[piece])
    for c in copies:
        c.wait_recv()
    sent += copies
    for q in range(gn):
        g_out[rows * q : rows * q + rows, :] = ag[q]
    for c in sent + x_copies:
        c.wait_send()
    s_copy.wait()


def gather(xn, data, reg, prev, low, sens, src, touched, couple, cmap, grad, gmap):
    zn = lax.axis_size("dev") // xn
    rn = lax.axis_size("region")
    n = data.shape[0]
    nbl, kk = sens.shape[0], sens.shape[1]
    kc, kg = couple.shape[1], grad.shape[1]
    dbl = data.shape[1] // BLK
    gn, yn, dn = 2 * xn, rn // 2, xn * zn
    rows = n // gn
    most = max(gn, zn, yn) - 1
    vm = pl.BlockSpec(memory_space=pltpu.VMEM)
    sm = pl.BlockSpec(memory_space=pltpu.SMEM)
    hbm = pl.BlockSpec(memory_space=pl.ANY)
    sem = pltpu.SemaphoreType.DMA
    width = nbl * BLK
    sizes = (xn, zn, rn, nbl, dbl, kk, kc, kg)
    row = touched.reshape(1, dn)
    return pl.pallas_call(
        functools.partial(gather_kernel, sizes),
        out_shape=(
            jax.ShapeDtypeStruct((SLICES * n, width), BF16),
            jax.ShapeDtypeStruct((n, BLK), F32),
        ),
        in_specs=[hbm, hbm, hbm, vm, hbm, sm, hbm, sm, hbm, sm, hbm, sm],
        out_specs=(hbm, vm),
        scratch_shapes=[
            tuple(pltpu.VMEM((dbl, n, BLK), BF16) for _ in range(zn)),
            pltpu.VMEM((dn, n, BLK), BF16),
            pltpu.VMEM((max(xn - 1, 1), zn, n, BLK), BF16),
            pltpu.VMEM((2 * dbl, n, BLK), BF16),
            pltpu.VMEM((nbl + 2, n, BLK), BF16),
            pltpu.VMEM((n, width), F32),
            pltpu.VMEM(sens.shape, BF16),
            pltpu.VMEM(couple.shape, BF16),
            pltpu.VMEM(grad.shape, BF16),
            pltpu.SMEM((max(xn - 1, 1), 1, dn), jnp.int32),
            pltpu.VMEM((n, width), F32),
            pltpu.VMEM((SLICES * n, width), BF16),
            pltpu.VMEM((gn, rows, BLK), F32),
            pltpu.VMEM((gn, rows, BLK), F32),
            pltpu.VMEM((zn, rows, BLK), F32),
            pltpu.VMEM((yn, rows, BLK), F32),
            pltpu.VMEM((gn, rows, BLK), F32),
            sem((dbl + nbl + 5,)),
            sem((2, zn // 2)),
            sem((2, zn // 2)),
            sem((xn, zn)),
            sem((xn, zn)),
            sem((4,)),
            sem((4,)),
            sem((xn,)),
            sem((xn,)),
            sem((4, most)),
            sem((4, most)),
        ],
        compiler_params=pltpu.CompilerParams(
            collective_id=0, has_side_effects=True, vmem_limit_bytes=40 * 2**20
        ),
        name="gather",
    )(data, reg, prev, low, row, touched, sens, src, couple, cmap, grad, gmap)


def local(
    data_panel, reg_panel, prev_panel, lower_block, sens_tiles, sens_src, touched,
    couple_tiles, couple_map, grad_tiles, grad_map,
):
    s, g = gather(
        X_CHIPS, data_panel, reg_panel, prev_panel, lower_block, sens_tiles, sens_src, touched,
        couple_tiles, couple_map, grad_tiles, grad_map,
    )
    return finish(g, s)


def solution(mesh):
    return jax.shard_map(
        local,
        mesh=mesh,
        in_specs=(
            P(None, ("region", "dev")),
            P(None, ("region", "dev")),
            P(None, ("region", "dev")),
            P(),
            P(("region", "dev"), None, None, None),
            P(("region", "dev"), None),
            P(("region", "dev")),
            P(("region", "dev"), None, None, None),
            P(("region", "dev"), None),
            P(("region", "dev"), None, None, None),
            P(("region", "dev"), None),
        ),
        out_specs=(P(None, ("region", "dev")), P()),
        check_vma=False,
    )
```

time: 343 us -> 72.2 us (0.21)
  blocking collectives: 195 us -> 0 us
  Pallas kernels: 0 us -> 61 us
  waiting for transfers between devices: 60.9 us -> 0 us
  other arithmetic: 28.9 us -> 0 us
  starting transfers between devices: 19.2 us -> 0 us
  between operations: 14.3 us -> 0.65 us
  matrix products: 7.56 us -> 0 us
  local copies, waits for them, and re-layouts: 16.6 us -> 10.1 us
    psum x2 -> x0, blocking collectives: 195 us -> none  [summed_gram(): return lax.psum(local_gram, ('region', 'dev'))]
    pallas_call x0 -> x2, Pallas kernels: none -> 61 us  [the longest x1 55.6 us: gather(): pl.pallas_call(functools.partial(gather_kernel, sizes), out_shape=(jax.Sh...]
    all_gather x1 -> x0, waiting for transfers between devices: 60.2 us -> none  [local(): lax.all_gather(data_panel, 'dev', axis=1, tiled=True)]
    another operation x10 -> x0, other arithmetic: 24.3 us -> none  [the longest x6 13.1 us: cholesky_pass(): lower_factor = jnp.linalg.cholesky(gram_sum)]
    ppermute x4 -> x0, starting transfers between devices: 19.2 us -> none  [the longest x2 12.7 us: extended_2(): lax.ppermute(lax.slice_in_dim(block, 0, width, axis=dim), axis, backward)]
    reshape x2 -> x0, local copies, waits for them, and re-layouts: 9.76 us -> none  [local(): lax.all_gather(data_panel, 'dev', axis=1, tiled=True)]
    unnamed x10 -> x20, local copies, waits for them, and re-layouts: 0.42 us -> 10.1 us
    dot_general x9 -> x0, matrix products: 7.06 us -> none  [the longest x3 2.36 us: tile_product(): lax.dot_general(picked, tiles, (((2, 3), (1, 2)), ((1,), (0,))), preferre...]
  transfers between devices with their start and end apart: 5 -> 0, of which waited for: 1 -> 0; matrix products, arithmetic and copies ran while one was open for 2% -> 0% of each run, Pallas kernels for 0% -> 0%
where the time goes in v1:
time: 72.2 us; the launch traced here: 71.7 us
  Pallas kernels  61 us (84%)
  local copies, waits for them, and re-layouts  10.1 us (14%)
    pallas_call x1, Pallas kernels, gather(): pl.pallas_call(functools.partial(gather_kernel, sizes), out_shape=(jax.Sh...  55.6 us
    unnamed x20, local copies, waits for them, and re-layouts  10.1 us
    pallas_call x1, Pallas kernels, finish(): pl.pallas_call(finish_kernel, out_shape=(jax.ShapeDtypeStruct((64, 1024),...  5.33 us

profile of v1, /device:TPU:1, one launch (start us, length us, event | category | flops | bytes accessed | tf_op | source)
XLA Modules:
  0.0 71.7 jit_solution(10000920140685765544)
XLA Ops:
  0.6 0.8 %copy.13.cmap = s32[8,2]{1,0:T(8,128)S(1)} copy(s32[8,2]{0,1:T(2,128)} %param.19) | data formatting | bytes 128 | tf_op args[8]
  1.4 0.8 %copy.14.gmap = s32[8,3]{1,0:T(8,128)S(1)} copy(s32[8,3]{0,1:T(4,128)} %param.21) | data formatting | bytes 192 | tf_op args[10]
  2.1 0.0 copy-start
  2.1 1.6 %copy-done = bf16[8,8,128,128]{3,2,1,0:T(8,128)(2,1)S(1)} copy-done((bf16[8,8,128,128]{3,2,1,0:T(8,128)(2,1)S(1)}, bf16[8,8,128,128]{3,2,1,0:T(8,128)(2,1)}, u32[]{:S(2)}) %copy-start) | copy-done | bytes 2097176
  3.7 0.0 copy-start.1
  3.7 1.1 %copy-done.1 = bf16[8,3,128,128]{3,2,1,0:T(8,128)(2,1)S(1)} copy-done((bf16[8,3,128,128]{3,2,1,0:T(8,128)(2,1)S(1)}, bf16[8,3,128,128]{3,2,1,0:T(8,128)(2,1)}, u32[]{:S(2)}) %copy-start.1) | copy-done | bytes 786456
  4.9 0.0 copy-start.2
  4.9 1.0 %copy-done.2 = bf16[8,2,128,128]{3,2,1,0:T(8,128)(2,1)S(1)} copy-done((bf16[8,2,128,128]{3,2,1,0:T(8,128)(2,1)S(1)}, bf16[8,2,128,128]{3,2,1,0:T(8,128)(2,1)}, u32[]{:S(2)}) %copy-start.2) | copy-done | bytes 524312
  5.9 0.0 copy-start.3
  5.9 0.9 %copy-done.3 = f32[64,1024]{1,0:T(8,128)S(1)} copy-done((f32[64,1024]{1,0:T(8,128)S(1)}, f32[64,1024]{1,0:T(8,128)}, u32[]{:S(2)}) %copy-start.3) | copy-done | bytes 262168
  6.9 0.0 copy-start.4
  6.9 0.9 %copy-done.4 = bf16[64,1024]{1,0:T(8,128)(2,1)S(1)} copy-done((bf16[64,1024]{1,0:T(8,128)(2,1)S(1)}, bf16[64,1024]{1,0:T(8,128)(2,1)}, u32[]{:S(2)}) %copy-start.4) | copy-done | bytes 131096
  7.8 0.0 copy-start.5
  7.8 0.8 %copy-done.5 = bf16[64,512]{1,0:T(8,128)(2,1)S(1)} copy-done((bf16[64,512]{1,0:T(8,128)(2,1)S(1)}, bf16[64,512]{1,0:T(8,128)(2,1)}, u32[]{:S(2)}) %copy-start.5) | copy-done | bytes 65560
  8.6 0.0 copy-start.6
  8.6 0.8 %copy-done.6 = f32[64,64]{1,0:T(8,128)S(1)} copy-done((f32[64,64]{1,0:T(8,128)S(1)}, f32[64,64]{1,0:T(8,128)}, u32[]{:S(2)}) %copy-start.6) | copy-done | bytes 16408
  9.4 0.0 copy-start.7
  9.4 0.7 copy-done.7
  10.0 0.0 copy-start.8
  10.1 0.7 copy-done.8
  10.7 55.6 %gather.1 = (bf16[256,1024]{1,0:T(8,128)(2,1)S(1)}, f32[64,128]{1,0:T(8,128)S(1)}) custom-call(bf16[64,512]{1,0:T(8,128)(2,1)S(1)} %copy-done.5, bf16[64,1024]{1,0:T(8,128)(2,1)S(1)} %copy-done.4, f32[64,1024]{1,0:T(8,128)S(1)} %copy-done.3, f32[64,64]{1,0:T(8,128)S(1)} %copy-done.6, s32[1,32]{1,0:T(1,128)S(1)} %bitcast.1, s32[32]{0:T(128)S(1)} %copy-done.8, ...), custom_call_target="tpu_custom_call" | custom-call | tf_op jit(solution)/shard_map/gather/pallas_call | solution.py:413
  66.3 5.3 %finish.1 = (f32[64,1024]{1,0:T(8,128)}, f32[64,64]{1,0:T(8,128)}) custom-call(f32[64,128]{1,0:T(8,128)S(1)} %get-tuple-element.4.g_ref, bf16[256,1024]{1,0:T(8,128)(2,1)S(1)} %get-tuple-element.5.s_ref), custom_call_target="tpu_custom_call" | custom-call | tf_op jit(solution)/shard_map/finish/pallas_call | solution.py:124
Async XLA Ops:
  2.1 1.6 %copy-start = (bf16[8,8,128,128]{3,2,1,0:T(8,128)(2,1)S(1)}, bf16[8,8,128,128]{3,2,1,0:T(8,128)(2,1)}, u32[]{:S(2)}) copy-start(bf16[8,8,128,128]{3,2,1,0:T(8,128)(2,1)} %sens.1) | copy-start | bytes 6291460
  3.7 1.1 %copy-start.1 = (bf16[8,3,128,128]{3,2,1,0:T(8,128)(2,1)S(1)}, bf16[8,3,128,128]{3,2,1,0:T(8,128)(2,1)}, u32[]{:S(2)}) copy-start(bf16[8,3,128,128]{3,2,1,0:T(8,128)(2,1)} %grad.1) | copy-start | bytes 2359300
  4.9 1.0 %copy-start.2 = (bf16[8,2,128,128]{3,2,1,0:T(8,128)(2,1)S(1)}, bf16[8,2,128,128]{3,2,1,0:T(8,128)(2,1)}, u32[]{:S(2)}) copy-start(bf16[8,2,128,128]{3,2,1,0:T(8,128)(2,1)} %couple.1) | copy-start | bytes 1572868
  5.9 0.9 %copy-start.3 = (f32[64,1024]{1,0:T(8,128)S(1)}, f32[64,1024]{1,0:T(8,128)}, u32[]{:S(2)}) copy-start(f32[64,1024]{1,0:T(8,128)} %prev.1) | copy-start | bytes 786436
  6.9 0.9 %copy-start.4 = (bf16[64,1024]{1,0:T(8,128)(2,1)S(1)}, bf16[64,1024]{1,0:T(8,128)(2,1)}, u32[]{:S(2)}) copy-start(bf16[64,1024]{1,0:T(8,128)(2,1)} %reg.1) | copy-start | bytes 393220
  7.8 0.8 %copy-start.5 = (bf16[64,512]{1,0:T(8,128)(2,1)S(1)}, bf16[64,512]{1,0:T(8,128)(2,1)}, u32[]{:S(2)}) copy-start(bf16[64,512]{1,0:T(8,128)(2,1)} %data.1) | copy-start | bytes 196612
  8.6 0.8 %copy-start.6 = (f32[64,64]{1,0:T(8,128)S(1)}, f32[64,64]{1,0:T(8,128)}, u32[]{:S(2)}) copy-start(f32[64,64]{1,0:T(8,128)} %low.1) | copy-start | bytes 49156
  9.4 0.7 copy-start.7
  10.0 0.7 copy-start.8

commit v2 on v1

--- a/solution.py
+++ b/solution.py
@@ -63,8 +63,10 @@
     return hi, mid, (r - mid.astype(F32)).astype(BF16)
 
 
-def finish_kernel(g_ref, s_ref, q_ref, f_ref):
+def finish_kernel(g_ref, s_any, q_ref, f_ref, s_ref, s_sem):
     n = 64
+    s_copy = pltpu.make_async_copy(s_any, s_ref, s_sem)
+    s_copy.start()
     g = g_ref[...]
     lane = lax.broadcasted_iota(jnp.int32, (n, 128), 1)
     subl = lax.broadcasted_iota(jnp.int32, (n, 128), 0)
@@ -114,6 +116,7 @@
     f_ref[...] = both
     m = jnp.dot(w2[:, :n], w[:, :n], precision=lax.Precision.HIGHEST, preferred_element_type=F32)
     parts = jnp.concatenate([jnp.concatenate([p] * SLICES, axis=1) for p in split3(m)], axis=0)
+    s_copy.wait()
     for c in range(4):
         res = jnp.dot(parts, s_ref[:, 256 * c : 256 * c + 256], preferred_element_type=F32)
         q_ref[:, 256 * c : 256 * c + 256] = res[:n] + (res[n : 2 * n] + res[2 * n :])
@@ -124,9 +127,10 @@
     return pl.pallas_call(
         finish_kernel,
         out_shape=(jax.ShapeDtypeStruct((64, 1024), F32), jax.ShapeDtypeStruct((64, 64), F32)),
-        in_specs=[vm, vm],
+        in_specs=[vm, pl.BlockSpec(memory_space=pltpu.HBM)],
         out_specs=(vm, vm),
-        compiler_params=pltpu.CompilerParams(vmem_limit_bytes=32 * 2**20),
+        scratch_shapes=[pltpu.VMEM(s.shape, BF16), pltpu.SemaphoreType.DMA(())],
+        compiler_params=pltpu.CompilerParams(vmem_limit_bytes=60 * 2**20),
         name="finish",
     )(g, s)
 
@@ -162,9 +166,9 @@
 
 def gather_kernel(
     sizes,
-    data, reg, prev, low, touched_any, touched, sens, src, couple, cmap, grad, gmap,
+    data, reg, prev, low_any, touched_any, sens, src_any, couple, cmap_any, grad, gmap_any,
     s_out, g_out,
-    zbs, compact, xs, nb, ext, prev_v, sens_v, couple_v, grad_v, asked, adj, s_v, gpart, rs, zs, ys, ag,
+    zbs, compact, xs, side, nb, ext, prev_v, low, sens_v, couple_v, grad_v, touched, src, cmap, gmap, asked, adj, s_v, gpart, rs, zs, ys, ag,
     l_sem, z_send, z_recv, x_send, x_recv, n_send, n_recv, t_send, t_recv, a_send, a_recv,
 ):
     xn, zn, rn, nbl, dbl, kk, kc, kg = sizes
@@ -194,7 +198,9 @@
 
     own = [fetch(data.at[:, pl.ds(BLK * b, BLK)], mine.at[b]) for b in range(dbl)]
     rim = [fetch(reg.at[:, pl.ds(BLK * b, BLK)], ext.at[b + 1]) for b in range(nbl)]
+    maps = [fetch(a, b) for a, b in ((touched_any, touched), (src_any, src), (cmap_any, cmap), (gmap_any, gmap))]
     prev_c = fetch(prev, prev_v)
+    low_c = fetch(low_any, low)
     grad_c = fetch(grad, grad_v)
     couple_c = fetch(couple, couple_v)
     sens_c = fetch(sens, sens_v)
@@ -216,7 +222,7 @@
     g = r * dn + d
     g_up, g_down = (g + 1) % (rn * dn), (g + rn * dn - 1) % (rn * dn)
     after, before = (g_up // dn, g_up % dn), (g_down // dn, g_down % dn)
-    reached = [group(o) for o in range(1, gn)] + [along_z(o) for o in range(1, zn)]
+    reached = [group(o) for o in range(1, gn)] + [along_z(1), along_z(zn - 1)]
     reached += [along_y(o) for o in range(1, yn)] + [up, down, after, before]
     barrier = pltpu.get_barrier_semaphore()
     for who in reached:
@@ -236,21 +242,16 @@
     for o in range(1, xn):
         asks.append(remote(touched_any, asked.at[xn - o - 1], t_send.at[o - 1], t_recv.at[o - 1], along_x(o)))
     sent += asks
-    for c in own:
-        c.wait()
-
-    def ring(step):
-        mid = dbl // 2
-        if step < half - 1:
-            pairs = [(below[step], below[step + 1]), (above[step], above[step + 1])]
-        else:
-            low_half, high_half = pl.ds(0, mid), pl.ds(mid, dbl - mid)
-            pairs = [(below[step].at[low_half], across.at[low_half]), (above[step].at[high_half], across.at[high_half])]
-        return [
-            remote(source, target, z_send.at[way, step], z_recv.at[way, step], along_z(1 if way == 0 else zn - 1))
-            for way, (source, target) in enumerate(pairs)
-        ]
-
+    def pass_on(way, step, b):
+        held = (below, above)[way]
+        target = held[step + 1] if step < half - 1 else across
+        source = data.at[:, pl.ds(BLK * b, BLK)] if step == 0 else held[step].at[b]
+        c = remote(source, target.at[b], z_send.at[way, step, b], z_recv.at[way, step, b],
+                   along_z(1 if way == 0 else zn - 1))
+        sent.append(c)
+        moves[way, step, b] = c
+
+    moves = {}
     x_copies = []
 
     def hand_on(slot, zz, held):
@@ -260,49 +261,59 @@
                 remote(xs.at[o - 1, slot], compact.at[zz * xn + x],
                        x_send.at[o - 1, slot], x_recv.at[o - 1, slot], along_x(o))
             )
-        compact[zz * xn + x] = held[touched[zz * xn + x]]
-
-    moves = ring(0)
-    sent += moves
-    for c in rim:
-        c.wait()
+        compact[zz * xn + x] = held[touched[0, zz * xn + x]]
+
+    for b in range(dbl):
+        for way in range(2):
+            if half > 1 or b // (dbl // 2) == way:
+                pass_on(way, 0, b)
     near = [
-        remote(mine, nb.at[pl.ds(0, dbl)], n_send.at[0], n_recv.at[0], up),
-        remote(mine, nb.at[pl.ds(dbl, dbl)], n_send.at[1], n_recv.at[1], down),
-        remote(ext.at[nbl], ext.at[0], n_send.at[2], n_recv.at[2], after),
-        remote(ext.at[1], ext.at[nbl + 1], n_send.at[3], n_recv.at[3], before),
+        remote(data, side[0], n_send.at[0], n_recv.at[0], up),
+        remote(data, side[1], n_send.at[1], n_recv.at[1], down),
+        remote(reg.at[:, pl.ds(BLK * (nbl - 1), BLK)], ext.at[0], n_send.at[2], n_recv.at[2], after),
+        remote(reg.at[:, pl.ds(0, BLK)], ext.at[nbl + 1], n_send.at[3], n_recv.at[3], before),
     ]
     sent += near
-    for c in asks:
-        c.wait_recv()
-    hand_on(0, z, mine)
-
-    prev_c.wait()
-    adj[...] = -jnp.dot(low[...], prev_v[...], precision=lax.Precision.HIGHEST, preferred_element_type=F32)
 
     def gradient(first, last):
         for b in range(first, last):
-            lhs = jnp.concatenate([ext[gmap[b, j]] for j in range(kg)], axis=1)
+            lhs = jnp.concatenate([ext[gmap[j, b]] for j in range(kg)], axis=1)
             part = jnp.dot(lhs, grad_v[b].reshape(kg * BLK, BLK), preferred_element_type=F32)
             adj[:, BLK * b : BLK * b + BLK] += 0.5 * part
 
     def coupling(first, last):
         for b in range(first, last):
-            lhs = jnp.concatenate([nb[cmap[b, j]] for j in range(kc)], axis=1)
+            lhs = jnp.concatenate([nb[cmap[j, b]] for j in range(kc)], axis=1)
             part = jnp.dot(lhs, couple_v[b].reshape(kc * BLK, BLK), preferred_element_type=F32)
             adj[:, BLK * b : BLK * b + BLK] += part
 
     for step in range(half):
-        for c in moves:
-            c.wait_recv()
+        for b in range(dbl):
+            for way in range(2):
+                if (way, step, b) in moves:
+                    moves[way, step, b].wait_recv()
+                    if step < half - 2 or (step == half - 2 and b // (dbl // 2) == way):
+                        pass_on(way, step + 1, b)
+        if step == 0:
+            for c in own + maps:
+                c.wait()
+            for c in asks:
+                c.wait_recv()
+            hand_on(0, z, mine)
         if step < half - 1:
-            moves = ring(step + 1)
-            sent += moves
             hand_on(2 * step + 1, (z + zn - step - 1) % zn, below[step + 1])
             hand_on(2 * step + 2, (z + step + 1) % zn, above[step + 1])
         else:
             hand_on(zn - 1, (z + half) % zn, across)
         if step == 0:
+            prev_c.wait()
+            low_c.wait()
+            adj[...] = -jnp.dot(
+                low[...], prev_v[...], precision=lax.Precision.HIGHEST, preferred_element_type=F32
+            )
+        if step == min(1, half - 1):
+            for c in rim:
+                c.wait()
             grad_c.wait()
             couple_c.wait()
             for c in near:
@@ -316,14 +327,10 @@
             def _():
                 ext[nbl + 1] = jnp.zeros((n, BLK), BF16)
 
-            @pl.when(r == 0)
-            def _():
-                nb[pl.ds(0, dbl)] = jnp.zeros((dbl, n, BLK), BF16)
-
-            @pl.when(r == rn - 1)
-            def _():
-                nb[pl.ds(dbl, dbl)] = jnp.zeros((dbl, n, BLK), BF16)
-
+            for k, edge in ((0, 0), (1, rn - 1)):
+                for b in range(dbl):
+                    block = side[k][:, BLK * b : BLK * b + BLK]
+                    nb[k * dbl + b] = jnp.where(r == edge, jnp.zeros_like(block), block)
             gradient(0, nbl)
             coupling(0, nbl)
     sens_c.wait()
@@ -338,25 +345,28 @@
     s_v[...] = s
     s_copy = fetch(s_v, s_out)
     gram = gram * (1.0 / (rn * dn * nbl * BLK))
+    lane = lax.broadcasted_iota(jnp.int32, (n // 2, BLK), 1)
+    swapped = pltpu.roll(gram, n, 1)
+    top, bottom = pl.ds(0, rows // 2), pl.ds(rows // 2, rows // 2)
+    gram_hi = jnp.where(lane < n, gram[: n // 2], swapped[n // 2 :])
+    gram_lo = jnp.where(lane < n, swapped[: n // 2], gram[n // 2 :])
     for q in range(gn):
-        gpart[q] = gram[rows * q : rows * q + rows, :]
-
-    lane = lax.broadcasted_iota(jnp.int32, (rows, BLK), 1)
-
-    def total(ref, count):
-        hi = ref[0]
-        lo = jnp.zeros_like(hi)
-        for q in range(1, count):
-            hi, e = two_sum(hi, ref[q])
-            lo = lo + e
-        lo = jnp.where(lane < n, lo, hi)
-        hi_part = hi
-        low_sum = pltpu.roll(lo, n, 1)
-        tail = jnp.where(lane < n, low_sum, 0.0) + jnp.where(lane < n, lo, 0.0)
-        top = jnp.where(lane < n, hi_part, 0.0)
-        big = top + tail
-        rest = tail - (big - top)
-        return jnp.where(lane < n, big, pltpu.roll(rest, n, 1))
+        part = slice(rows // 2 * q, rows // 2 * (q + 1))
+        gpart[q, top] = gram_hi[part]
+        gpart[q, bottom] = gram_lo[part]
+
+    def total(ref, count, target):
+        terms = [(ref[q, top], ref[q, bottom]) for q in range(count)]
+        while len(terms) > 1:
+            paired = []
+            for (a, a_low), (b, b_low) in zip(terms[::2], terms[1::2]):
+                hi, e = two_sum(a, b)
+                paired.append((hi, (a_low + b_low) + e))
+            terms = paired + terms[len(paired) * 2 :]
+        hi, lo = terms[0]
+        big = hi + lo
+        target[top] = big
+        target[bottom] = lo - (big - hi)
 
     def exchange(stage, count, mine, box, who, source):
         copies = []
@@ -371,23 +381,25 @@
     for c in copies:
         c.wait_recv()
     sent += copies
-    zs[z] = total(rs, gn)
+    total(rs, gn, zs.at[z])
     copies = exchange(1, zn, z, zs, along_z, lambda o: zs.at[z])
     for c in copies:
         c.wait_recv()
     sent += copies
-    ys[y] = total(zs, zn)
+    total(zs, zn, ys.at[y])
     copies = exchange(2, yn, y, ys, along_y, lambda o: ys.at[y])
     for c in copies:
         c.wait_recv()
     sent += copies
-    ag[piece] = total(ys, yn)
+    total(ys, yn, ag.at[piece])
     copies = exchange(3, gn, piece, ag, group, lambda o: ag.at[piece])
     for c in copies:
         c.wait_recv()
     sent += copies
-    for q in range(gn):
-        g_out[rows * q : rows * q + rows, :] = ag[q]
+    hi = jnp.concatenate([ag[q, top] for q in range(gn)], axis=0)
+    lo = jnp.concatenate([ag[q, bottom] for q in range(gn)], axis=0)
+    g_out[: n // 2, :] = jnp.where(lane < n, hi, pltpu.roll(lo, n, 1))
+    g_out[n // 2 :, :] = jnp.where(lane < n, pltpu.roll(hi, n, 1), lo)
     for c in sent + x_copies:
         c.wait_send()
     s_copy.wait()
@@ -404,8 +416,7 @@
     rows = n // gn
     most = max(gn, zn, yn) - 1
     vm = pl.BlockSpec(memory_space=pltpu.VMEM)
-    sm = pl.BlockSpec(memory_space=pltpu.SMEM)
-    hbm = pl.BlockSpec(memory_space=pl.ANY)
+    hbm = pl.BlockSpec(memory_space=pltpu.HBM)
     sem = pltpu.SemaphoreType.DMA
     width = nbl * BLK
     sizes = (xn, zn, rn, nbl, dbl, kk, kc, kg)
@@ -416,18 +427,24 @@
             jax.ShapeDtypeStruct((SLICES * n, width), BF16),
             jax.ShapeDtypeStruct((n, BLK), F32),
         ),
-        in_specs=[hbm, hbm, hbm, vm, hbm, sm, hbm, sm, hbm, sm, hbm, sm],
+        in_specs=[hbm] * 11,
         out_specs=(hbm, vm),
         scratch_shapes=[
             tuple(pltpu.VMEM((dbl, n, BLK), BF16) for _ in range(zn)),
             pltpu.VMEM((dn, n, BLK), BF16),
             pltpu.VMEM((max(xn - 1, 1), zn, n, BLK), BF16),
+            tuple(pltpu.VMEM((n, dbl * BLK), BF16) for _ in range(2)),
             pltpu.VMEM((2 * dbl, n, BLK), BF16),
             pltpu.VMEM((nbl + 2, n, BLK), BF16),
             pltpu.VMEM((n, width), F32),
+            pltpu.VMEM((n, n), F32),
             pltpu.VMEM(sens.shape, BF16),
             pltpu.VMEM(couple.shape, BF16),
             pltpu.VMEM(grad.shape, BF16),
+            pltpu.SMEM((1, dn), jnp.int32),
+            pltpu.SMEM((nbl, kk), jnp.int32),
+            pltpu.SMEM((kc, nbl), jnp.int32),
+            pltpu.SMEM((kg, nbl), jnp.int32),
             pltpu.SMEM((max(xn - 1, 1), 1, dn), jnp.int32),
             pltpu.VMEM((n, width), F32),
             pltpu.VMEM((SLICES * n, width), BF16),
@@ -436,9 +453,9 @@
             pltpu.VMEM((zn, rows, BLK), F32),
             pltpu.VMEM((yn, rows, BLK), F32),
             pltpu.VMEM((gn, rows, BLK), F32),
-            sem((dbl + nbl + 5,)),
-            sem((2, zn // 2)),
-            sem((2, zn // 2)),
+            sem((dbl + nbl + 10,)),
+            sem((2, zn // 2, dbl)),
+            sem((2, zn // 2, dbl)),
             sem((xn, zn)),
             sem((xn, zn)),
             sem((4,)),
@@ -449,10 +466,10 @@
             sem((4, most)),
         ],
         compiler_params=pltpu.CompilerParams(
-            collective_id=0, has_side_effects=True, vmem_limit_bytes=40 * 2**20
+            collective_id=0, has_side_effects=True, vmem_limit_bytes=60 * 2**20
         ),
         name="gather",
-    )(data, reg, prev, low, row, touched, sens, src, couple, cmap, grad, gmap)
+    )(data, reg, prev, low, row, sens, src, couple, cmap.T, grad, gmap.T)
 
 
 def local(

time: 72.2 us -> 59.4 us (0.82)
  local copies, waits for them, and re-layouts: 10.1 us -> 0 us
  Pallas kernels: 61 us -> 58.5 us
    unnamed x20 -> x0, local copies, waits for them, and re-layouts: 10.1 us -> none
    pallas_call x1, Pallas kernels: 55.6 us -> 52 us  [gather(): pl.pallas_call(functools.partial(gather_kernel, sizes), out_shape=(jax.Sh...]
    pallas_call x1, Pallas kernels: 5.33 us -> 6.51 us  [finish(): pl.pallas_call(finish_kernel, out_shape=(jax.ShapeDtypeStruct((64, 1024),...]
where the time goes in v2:
time: 59.4 us; the launch traced here: 59.1 us
  Pallas kernels  58.5 us (98%)
  between operations  0.64 us (1%)
    pallas_call x1, Pallas kernels, gather(): pl.pallas_call(functools.partial(gather_kernel, sizes), out_shape=(jax.Sh...  52 us
    pallas_call x1, Pallas kernels, finish(): pl.pallas_call(finish_kernel, out_shape=(jax.ShapeDtypeStruct((64, 1024),...  6.51 us

profile of v2, /device:TPU:1, one launch (start us, length us, event | category | flops | bytes accessed | tf_op | source)
XLA Modules:
  0.0 59.1 jit_solution(7522315553058905516)
XLA Ops:
  0.6 52.0 %gather.1 = (bf16[256,1024]{1,0:T(8,128)(2,1)}, f32[64,128]{1,0:T(8,128)}) custom-call(bf16[64,512]{1,0:T(8,128)(2,1)} %data.1, bf16[64,1024]{1,0:T(8,128)(2,1)} %reg.1, f32[64,1024]{1,0:T(8,128)} %prev.1, f32[64,64]{1,0:T(8,128)} %low_any.1, s32[1,32]{1,0:T(1,128)} %bitcast.5, bf16[8,8,128,128]{3,2,1,0:T(8,128)(2,1)} %sens.1, s32[8,8]{1,0:T(8,128)} %src_any.1, ...), custom_call_target="tpu_custom_call" | custom-call | tf_op jit(solution)/shard_map/gather/pallas_call | solution.py:424
  52.6 6.5 %finish.1 = (f32[64,1024]{1,0:T(8,128)}, f32[64,64]{1,0:T(8,128)}) custom-call(f32[64,128]{1,0:T(8,128)} %get-tuple-element.4.g_ref, bf16[256,1024]{1,0:T(8,128)(2,1)} %get-tuple-element.5.s_any), custom_call_target="tpu_custom_call" | custom-call | tf_op jit(solution)/shard_map/finish/pallas_call | solution.py:127

commit v3 on v2

--- a/solution.py
+++ b/solution.py
@@ -63,10 +63,8 @@
     return hi, mid, (r - mid.astype(F32)).astype(BF16)
 
 
-def finish_kernel(g_ref, s_any, q_ref, f_ref, s_ref, s_sem):
+def finish_kernel(g_ref, s_ref, q_ref, f_ref):
     n = 64
-    s_copy = pltpu.make_async_copy(s_any, s_ref, s_sem)
-    s_copy.start()
     g = g_ref[...]
     lane = lax.broadcasted_iota(jnp.int32, (n, 128), 1)
     subl = lax.broadcasted_iota(jnp.int32, (n, 128), 0)
@@ -116,7 +114,6 @@
     f_ref[...] = both
     m = jnp.dot(w2[:, :n], w[:, :n], precision=lax.Precision.HIGHEST, preferred_element_type=F32)
     parts = jnp.concatenate([jnp.concatenate([p] * SLICES, axis=1) for p in split3(m)], axis=0)
-    s_copy.wait()
     for c in range(4):
         res = jnp.dot(parts, s_ref[:, 256 * c : 256 * c + 256], preferred_element_type=F32)
         q_ref[:, 256 * c : 256 * c + 256] = res[:n] + (res[n : 2 * n] + res[2 * n :])
@@ -127,10 +124,9 @@
     return pl.pallas_call(
         finish_kernel,
         out_shape=(jax.ShapeDtypeStruct((64, 1024), F32), jax.ShapeDtypeStruct((64, 64), F32)),
-        in_specs=[vm, pl.BlockSpec(memory_space=pltpu.HBM)],
+        in_specs=[vm, vm],
         out_specs=(vm, vm),
-        scratch_shapes=[pltpu.VMEM(s.shape, BF16), pltpu.SemaphoreType.DMA(())],
-        compiler_params=pltpu.CompilerParams(vmem_limit_bytes=60 * 2**20),
+        compiler_params=pltpu.CompilerParams(vmem_limit_bytes=32 * 2**20),
         name="finish",
     )(g, s)
 
@@ -168,7 +164,7 @@
     sizes,
     data, reg, prev, low_any, touched_any, sens, src_any, couple, cmap_any, grad, gmap_any,
     s_out, g_out,
-    zbs, compact, xs, side, nb, ext, prev_v, low, sens_v, couple_v, grad_v, touched, src, cmap, gmap, asked, adj, s_v, gpart, rs, zs, ys, ag,
+    zbs, compact, xs, side, nb, ext, prev_v, low, sens_v, couple_v, grad_v, touched, src, cmap, gmap, asked, adj, gpart, rs, zs, ys, ag,
     l_sem, z_send, z_recv, x_send, x_recv, n_send, n_recv, t_send, t_recv, a_send, a_recv,
 ):
     xn, zn, rn, nbl, dbl, kk, kc, kg = sizes
@@ -188,6 +184,28 @@
     above = [mine] + list(zbs[half : 2 * half - 1])
     across = zbs[2 * half - 1]
 
+    def group(o):
+        q = (piece + o) % gn
+        return (y * 2 + q % 2, z * xn + q // 2)
+
+    def along_z(o):
+        return (r, ((z + o) % zn) * xn + x)
+
+    def along_y(o):
+        return (((y + o) % yn) * 2 + core, d)
+
+    def along_x(o):
+        return (r, z * xn + (x + o) % xn)
+
+    up, down = ((r + 1) % rn, d), ((r + rn - 1) % rn, d)
+    g = r * dn + d
+    g_up, g_down = (g + 1) % (rn * dn), (g + rn * dn - 1) % (rn * dn)
+    after, before = (g_up // dn, g_up % dn), (g_down // dn, g_down % dn)
+    reached = [group(o) for o in range(1, gn)] + [along_z(o) for o in range(1, zn) if min(o, zn - o) <= 2]
+    reached += [along_y(o) for o in range(1, yn)] + [up, down, after, before]
+    barrier = pltpu.get_barrier_semaphore()
+    for who in reached:
+        pl.semaphore_signal(barrier, inc=1, device_id=who, device_id_type=MESH)
     local = []
 
     def fetch(source, target):
@@ -205,28 +223,6 @@
     couple_c = fetch(couple, couple_v)
     sens_c = fetch(sens, sens_v)
 
-    def group(o):
-        q = (piece + o) % gn
-        return (y * 2 + q % 2, z * xn + q // 2)
-
-    def along_z(o):
-        return (r, ((z + o) % zn) * xn + x)
-
-    def along_y(o):
-        return (((y + o) % yn) * 2 + core, d)
-
-    def along_x(o):
-        return (r, z * xn + (x + o) % xn)
-
-    up, down = ((r + 1) % rn, d), ((r + rn - 1) % rn, d)
-    g = r * dn + d
-    g_up, g_down = (g + 1) % (rn * dn), (g + rn * dn - 1) % (rn * dn)
-    after, before = (g_up // dn, g_up % dn), (g_down // dn, g_down % dn)
-    reached = [group(o) for o in range(1, gn)] + [along_z(1), along_z(zn - 1)]
-    reached += [along_y(o) for o in range(1, yn)] + [up, down, after, before]
-    barrier = pltpu.get_barrier_semaphore()
-    for who in reached:
-        pl.semaphore_signal(barrier, inc=1, device_id=who, device_id_type=MESH)
     pl.semaphore_wait(barrier, len(reached))
 
     def remote(source, target, send, recv, who):
@@ -242,14 +238,18 @@
     for o in range(1, xn):
         asks.append(remote(touched_any, asked.at[xn - o - 1], t_send.at[o - 1], t_recv.at[o - 1], along_x(o)))
     sent += asks
-    def pass_on(way, step, b):
+    def pass_on(way, far, b):
         held = (below, above)[way]
-        target = held[step + 1] if step < half - 1 else across
-        source = data.at[:, pl.ds(BLK * b, BLK)] if step == 0 else held[step].at[b]
-        c = remote(source, target.at[b], z_send.at[way, step, b], z_recv.at[way, step, b],
-                   along_z(1 if way == 0 else zn - 1))
+        target = held[far] if far < half else across
+        hops = far if far <= 2 else far - 2
+        source = (mine if far <= 2 else held[2]).at[b]
+        c = remote(source, target.at[b], z_send.at[way, far - 1, b], z_recv.at[way, far - 1, b],
+                   along_z(hops if way == 0 else zn - hops))
         sent.append(c)
-        moves[way, step, b] = c
+        moves[way, far, b] = c
+
+    def parts(far):
+        return [(way, b) for b in range(dbl) for way in range(2) if far < half or b // (dbl // 2) == way]
 
     moves = {}
     x_copies = []
@@ -263,10 +263,11 @@
             )
         compact[zz * xn + x] = held[touched[0, zz * xn + x]]
 
-    for b in range(dbl):
-        for way in range(2):
-            if half > 1 or b // (dbl // 2) == way:
-                pass_on(way, 0, b)
+    for c in own:
+        c.wait()
+    for far in range(min(2, half), 0, -1):
+        for way, b in parts(far):
+            pass_on(way, far, b)
     near = [
         remote(data, side[0], n_send.at[0], n_recv.at[0], up),
         remote(data, side[1], n_send.at[1], n_recv.at[1], down),
@@ -287,52 +288,59 @@
             part = jnp.dot(lhs, couple_v[b].reshape(kc * BLK, BLK), preferred_element_type=F32)
             adj[:, BLK * b : BLK * b + BLK] += part
 
-    for step in range(half):
-        for b in range(dbl):
-            for way in range(2):
-                if (way, step, b) in moves:
-                    moves[way, step, b].wait_recv()
-                    if step < half - 2 or (step == half - 2 and b // (dbl // 2) == way):
-                        pass_on(way, step + 1, b)
-        if step == 0:
-            for c in own + maps:
-                c.wait()
-            for c in asks:
-                c.wait_recv()
-            hand_on(0, z, mine)
-        if step < half - 1:
-            hand_on(2 * step + 1, (z + zn - step - 1) % zn, below[step + 1])
-            hand_on(2 * step + 2, (z + step + 1) % zn, above[step + 1])
+    def arrive(far):
+        for way, b in parts(far):
+            moves[way, far, b].wait_recv()
+            if far == 2:
+                for further in range(half, 2, -1):
+                    if (way, b) in parts(further):
+                        pass_on(way, further, b)
+
+    def hand_on_far(far):
+        if far < half:
+            hand_on(2 * far - 1, (z + zn - far) % zn, below[far])
+            hand_on(2 * far, (z + far) % zn, above[far])
         else:
             hand_on(zn - 1, (z + half) % zn, across)
-        if step == 0:
-            prev_c.wait()
-            low_c.wait()
-            adj[...] = -jnp.dot(
-                low[...], prev_v[...], precision=lax.Precision.HIGHEST, preferred_element_type=F32
-            )
-        if step == min(1, half - 1):
-            for c in rim:
-                c.wait()
-            grad_c.wait()
-            couple_c.wait()
-            for c in near:
-                c.wait_recv()
-
-            @pl.when(g == 0)
-            def _():
-                ext[0] = jnp.zeros((n, BLK), BF16)
-
-            @pl.when(g == rn * dn - 1)
-            def _():
-                ext[nbl + 1] = jnp.zeros((n, BLK), BF16)
-
-            for k, edge in ((0, 0), (1, rn - 1)):
-                for b in range(dbl):
-                    block = side[k][:, BLK * b : BLK * b + BLK]
-                    nb[k * dbl + b] = jnp.where(r == edge, jnp.zeros_like(block), block)
-            gradient(0, nbl)
-            coupling(0, nbl)
+
+    for far in range(min(2, half), 0, -1):
+        arrive(far)
+    for c in maps:
+        c.wait()
+    for c in asks:
+        c.wait_recv()
+    hand_on(0, z, mine)
+    for far in range(1, min(2, half) + 1):
+        hand_on_far(far)
+    prev_c.wait()
+    low_c.wait()
+    adj[...] = -jnp.dot(
+        low[...], prev_v[...], precision=lax.Precision.HIGHEST, preferred_element_type=F32
+    )
+    for c in rim:
+        c.wait()
+    grad_c.wait()
+    couple_c.wait()
+    for c in near:
+        c.wait_recv()
+
+    @pl.when(g == 0)
+    def _():
+        ext[0] = jnp.zeros((n, BLK), BF16)
+
+    @pl.when(g == rn * dn - 1)
+    def _():
+        ext[nbl + 1] = jnp.zeros((n, BLK), BF16)
+
+    for k, edge in ((0, 0), (1, rn - 1)):
+        for b in range(dbl):
+            block = side[k][:, BLK * b : BLK * b + BLK]
+            nb[k * dbl + b] = jnp.where(r == edge, jnp.zeros_like(block), block)
+    gradient(0, nbl)
+    coupling(0, nbl)
+    for far in range(3, half + 1):
+        arrive(far)
+        hand_on_far(far)
     sens_c.wait()
     for c in x_copies:
         c.wait_recv()
@@ -342,8 +350,7 @@
         adj[:, BLK * b : BLK * b + BLK] += part
 
     s, gram = gram_local(adj[...])
-    s_v[...] = s
-    s_copy = fetch(s_v, s_out)
+    s_out[...] = s
     gram = gram * (1.0 / (rn * dn * nbl * BLK))
     lane = lax.broadcasted_iota(jnp.int32, (n // 2, BLK), 1)
     swapped = pltpu.roll(gram, n, 1)
@@ -402,7 +409,6 @@
     g_out[n // 2 :, :] = jnp.where(lane < n, pltpu.roll(hi, n, 1), lo)
     for c in sent + x_copies:
         c.wait_send()
-    s_copy.wait()
 
 
 def gather(xn, data, reg, prev, low, sens, src, touched, couple, cmap, grad, gmap):
@@ -424,11 +430,11 @@
     return pl.pallas_call(
         functools.partial(gather_kernel, sizes),
         out_shape=(
-            jax.ShapeDtypeStruct((SLICES * n, width), BF16),
-            jax.ShapeDtypeStruct((n, BLK), F32),
+            pltpu.VMEM((SLICES * n, width), BF16),
+            pltpu.VMEM((n, BLK), F32),
         ),
         in_specs=[hbm] * 11,
-        out_specs=(hbm, vm),
+        out_specs=(vm, vm),
         scratch_shapes=[
             tuple(pltpu.VMEM((dbl, n, BLK), BF16) for _ in range(zn)),
             pltpu.VMEM((dn, n, BLK), BF16),
@@ -447,7 +453,6 @@
             pltpu.SMEM((kg, nbl), jnp.int32),
             pltpu.SMEM((max(xn - 1, 1), 1, dn), jnp.int32),
             pltpu.VMEM((n, width), F32),
-            pltpu.VMEM((SLICES * n, width), BF16),
             pltpu.VMEM((gn, rows, BLK), F32),
             pltpu.VMEM((gn, rows, BLK), F32),
             pltpu.VMEM((zn, rows, BLK), F32),

time: 59.4 us -> 55 us (0.926)
  Pallas kernels: 58.5 us -> 54.2 us
    pallas_call x1, Pallas kernels: 52 us -> 48.9 us  [gather(): pl.pallas_call(functools.partial(gather_kernel, sizes), out_shape=(pltpu....]
    pallas_call x1, Pallas kernels: 6.51 us -> 5.33 us  [finish(): pl.pallas_call(finish_kernel, out_shape=(jax.ShapeDtypeStruct((64, 1024),...]
where the time goes in v3:
time: 55 us; the launch traced here: 54.9 us
  Pallas kernels  54.2 us (99%)
  between operations  0.64 us (1%)
    pallas_call x1, Pallas kernels, gather(): pl.pallas_call(functools.partial(gather_kernel, sizes), out_shape=(pltpu....  48.9 us
    pallas_call x1, Pallas kernels, finish(): pl.pallas_call(finish_kernel, out_shape=(jax.ShapeDtypeStruct((64, 1024),...  5.33 us

profile of v3, /device:TPU:1, one launch (start us, length us, event | category | flops | bytes accessed | tf_op | source)
XLA Modules:
  0.0 54.9 jit_solution(11127640358938549826)
XLA Ops:
  0.6 48.9 %gather.1 = (bf16[256,1024]{1,0:T(8,128)(2,1)S(1)}, f32[64,128]{1,0:T(8,128)S(1)}) custom-call(bf16[64,512]{1,0:T(8,128)(2,1)} %data.1, bf16[64,1024]{1,0:T(8,128)(2,1)} %reg.1, f32[64,1024]{1,0:T(8,128)} %prev.1, f32[64,64]{1,0:T(8,128)} %low_any.1, s32[1,32]{1,0:T(1,128)} %bitcast.5, bf16[8,8,128,128]{3,2,1,0:T(8,128)(2,1)} %sens.1, s32[8,8]{1,0:T(8,128)} %src_any.1, ...), custom_call_target="tpu_custom_call" | custom-call | tf_op jit(solution)/shard_map/gather/pallas_call | solution.py:430
  49.5 5.3 %finish.1 = (f32[64,1024]{1,0:T(8,128)}, f32[64,64]{1,0:T(8,128)}) custom-call(f32[64,128]{1,0:T(8,128)S(1)} %get-tuple-element.4.g_ref, bf16[256,1024]{1,0:T(8,128)(2,1)S(1)} %get-tuple-element.5.s_ref), custom_call_target="tpu_custom_call" | custom-call | tf_op jit(solution)/shard_map/finish/pallas_call | solution.py:124

commit v4 on v3

--- a/solution.py
+++ b/solution.py
@@ -184,6 +184,16 @@
     above = [mine] + list(zbs[half : 2 * half - 1])
     across = zbs[2 * half - 1]
 
+    local = []
+
+    def fetch(source, target):
+        c = pltpu.make_async_copy(source, target, l_sem.at[len(local)])
+        c.start()
+        local.append(c)
+        return c
+
+    own = [fetch(data.at[:, pl.ds(BLK * b, BLK)], mine.at[b]) for b in range(dbl)]
+    maps = [fetch(a, b) for a, b in ((touched_any, touched), (src_any, src), (cmap_any, cmap), (gmap_any, gmap))]
     def group(o):
         q = (piece + o) % gn
         return (y * 2 + q % 2, z * xn + q // 2)
@@ -206,23 +216,6 @@
     barrier = pltpu.get_barrier_semaphore()
     for who in reached:
         pl.semaphore_signal(barrier, inc=1, device_id=who, device_id_type=MESH)
-    local = []
-
-    def fetch(source, target):
-        c = pltpu.make_async_copy(source, target, l_sem.at[len(local)])
-        c.start()
-        local.append(c)
-        return c
-
-    own = [fetch(data.at[:, pl.ds(BLK * b, BLK)], mine.at[b]) for b in range(dbl)]
-    rim = [fetch(reg.at[:, pl.ds(BLK * b, BLK)], ext.at[b + 1]) for b in range(nbl)]
-    maps = [fetch(a, b) for a, b in ((touched_any, touched), (src_any, src), (cmap_any, cmap), (gmap_any, gmap))]
-    prev_c = fetch(prev, prev_v)
-    low_c = fetch(low_any, low)
-    grad_c = fetch(grad, grad_v)
-    couple_c = fetch(couple, couple_v)
-    sens_c = fetch(sens, sens_v)
-
     pl.semaphore_wait(barrier, len(reached))
 
     def remote(source, target, send, recv, who):
@@ -303,14 +296,19 @@
         else:
             hand_on(zn - 1, (z + half) % zn, across)
 
-    for far in range(min(2, half), 0, -1):
-        arrive(far)
     for c in maps:
         c.wait()
     for c in asks:
         c.wait_recv()
     hand_on(0, z, mine)
-    for far in range(1, min(2, half) + 1):
+    rim = [fetch(reg.at[:, pl.ds(BLK * b, BLK)], ext.at[b + 1]) for b in range(nbl)]
+    prev_c = fetch(prev, prev_v)
+    low_c = fetch(low_any, low)
+    grad_c = fetch(grad, grad_v)
+    couple_c = fetch(couple, couple_v)
+    sens_c = fetch(sens, sens_v)
+    for far in range(min(2, half), 0, -1):
+        arrive(far)
         hand_on_far(far)
     prev_c.wait()
     low_c.wait()

time: 55 us -> 54.3 us (0.987)
  Pallas kernels: 54.2 us -> 53.5 us
    pallas_call x1, Pallas kernels: 48.9 us -> 48.2 us  [gather(): pl.pallas_call(functools.partial(gather_kernel, sizes), out_shape=(pltpu....]
where the time goes in v4:
time: 54.3 us; the launch traced here: 54.2 us
  Pallas kernels  53.5 us (99%)
  between operations  0.64 us (1%)
    pallas_call x1, Pallas kernels, gather(): pl.pallas_call(functools.partial(gather_kernel, sizes), out_shape=(pltpu....  48.2 us
    pallas_call x1, Pallas kernels, finish(): pl.pallas_call(finish_kernel, out_shape=(jax.ShapeDtypeStruct((64, 1024),...  5.33 us

profile of v4, /device:TPU:1, one launch (start us, length us, event | category | flops | bytes accessed | tf_op | source)
XLA Modules:
  0.0 54.2 jit_solution(9088386537114855517)
XLA Ops:
  0.6 48.2 %gather.1 = (bf16[256,1024]{1,0:T(8,128)(2,1)S(1)}, f32[64,128]{1,0:T(8,128)S(1)}) custom-call(bf16[64,512]{1,0:T(8,128)(2,1)} %data.1, bf16[64,1024]{1,0:T(8,128)(2,1)} %reg.1, f32[64,1024]{1,0:T(8,128)} %prev.1, f32[64,64]{1,0:T(8,128)} %low_any.1, s32[1,32]{1,0:T(1,128)} %bitcast.5, bf16[8,8,128,128]{3,2,1,0:T(8,128)(2,1)} %sens.1, s32[8,8]{1,0:T(8,128)} %src_any.1, ...), custom_call_target="tpu_custom_call" | custom-call | tf_op jit(solution)/shard_map/gather/pallas_call | solution.py:428
  48.8 5.3 %finish.1 = (f32[64,1024]{1,0:T(8,128)}, f32[64,64]{1,0:T(8,128)}) custom-call(f32[64,128]{1,0:T(8,128)S(1)} %get-tuple-element.4.g_ref, bf16[256,1024]{1,0:T(8,128)(2,1)S(1)} %get-tuple-element.5.s_ref), custom_call_target="tpu_custom_call" | custom-call | tf_op jit(solution)/shard_map/finish/pallas_call | solution.py:124

commit v5 on v4

--- a/solution.py
+++ b/solution.py
@@ -248,7 +248,7 @@
     x_copies = []
 
     def hand_on(slot, zz, held):
-        for o in range(1, xn):
+        for o in sorted(range(1, xn), key=lambda o: -min(o, xn - o)):
             xs[o - 1, slot] = held[asked[o - 1, 0, zz * xn + x]]
             x_copies.append(
                 remote(xs.at[o - 1, slot], compact.at[zz * xn + x],
@@ -375,7 +375,7 @@
 
     def exchange(stage, count, mine, box, who, source):
         copies = []
-        for o in range(1, count):
+        for o in sorted(range(1, count), key=lambda o: -min(o, count - o)):
             copies.append(
                 remote(source(o), box.at[mine], a_send.at[stage, o - 1], a_recv.at[stage, o - 1], who(o))
             )
@@ -383,29 +383,37 @@
 
     copies = exchange(0, gn, piece, rs, group, lambda o: gpart.at[(piece + o) % gn])
     rs[piece] = gpart[piece]
+    for c in sent + x_copies:
+        c.wait_send()
+    last = copies
     for c in copies:
         c.wait_recv()
-    sent += copies
     total(rs, gn, zs.at[z])
     copies = exchange(1, zn, z, zs, along_z, lambda o: zs.at[z])
+    for c in last:
+        c.wait_send()
+    last = copies
     for c in copies:
         c.wait_recv()
-    sent += copies
     total(zs, zn, ys.at[y])
     copies = exchange(2, yn, y, ys, along_y, lambda o: ys.at[y])
+    for c in last:
+        c.wait_send()
+    last = copies
     for c in copies:
         c.wait_recv()
-    sent += copies
     total(ys, yn, ag.at[piece])
     copies = exchange(3, gn, piece, ag, group, lambda o: ag.at[piece])
+    for c in last:
+        c.wait_send()
+    last = copies
     for c in copies:
         c.wait_recv()
-    sent += copies
     hi = jnp.concatenate([ag[q, top] for q in range(gn)], axis=0)
     lo = jnp.concatenate([ag[q, bottom] for q in range(gn)], axis=0)
     g_out[: n // 2, :] = jnp.where(lane < n, hi, pltpu.roll(lo, n, 1))
     g_out[n // 2 :, :] = jnp.where(lane < n, pltpu.roll(hi, n, 1), lo)
-    for c in sent + x_copies:
+    for c in last:
         c.wait_send()
 
 

time: 54.3 us -> 53.6 us (0.987)
  Pallas kernels: 53.5 us -> 52.8 us
    pallas_call x1, Pallas kernels: 48.2 us -> 47.5 us  [gather(): pl.pallas_call(functools.partial(gather_kernel, sizes), out_shape=(pltpu....]
where the time goes in v5:
time: 53.6 us; the launch traced here: 53.5 us
  Pallas kernels  52.8 us (99%)
  between operations  0.64 us (1%)
    pallas_call x1, Pallas kernels, gather(): pl.pallas_call(functools.partial(gather_kernel, sizes), out_shape=(pltpu....  47.5 us
    pallas_call x1, Pallas kernels, finish(): pl.pallas_call(finish_kernel, out_shape=(jax.ShapeDtypeStruct((64, 1024),...  5.33 us

profile of v5, /device:TPU:1, one launch (start us, length us, event | category | flops | bytes accessed | tf_op | source)
XLA Modules:
  0.0 53.5 jit_solution(11225356462055654688)
XLA Ops:
  0.6 47.5 %gather.1 = (bf16[256,1024]{1,0:T(8,128)(2,1)S(1)}, f32[64,128]{1,0:T(8,128)S(1)}) custom-call(bf16[64,512]{1,0:T(8,128)(2,1)} %data.1, bf16[64,1024]{1,0:T(8,128)(2,1)} %reg.1, f32[64,1024]{1,0:T(8,128)} %prev.1, f32[64,64]{1,0:T(8,128)} %low_any.1, s32[1,32]{1,0:T(1,128)} %bitcast.5, bf16[8,8,128,128]{3,2,1,0:T(8,128)(2,1)} %sens.1, s32[8,8]{1,0:T(8,128)} %src_any.1, ...), custom_call_target="tpu_custom_call" | custom-call | tf_op jit(solution)/shard_map/gather/pallas_call | solution.py:436
  48.2 5.3 %finish.1 = (f32[64,1024]{1,0:T(8,128)}, f32[64,64]{1,0:T(8,128)}) custom-call(f32[64,128]{1,0:T(8,128)S(1)} %get-tuple-element.4.g_ref, bf16[256,1024]{1,0:T(8,128)(2,1)S(1)} %get-tuple-element.5.s_ref), custom_call_target="tpu_custom_call" | custom-call | tf_op jit(solution)/shard_map/finish/pallas_call | solution.py:124
